TPU v7x, 256 devices: a whole 4x4x8 slice. The times are simulated.
256 devices in a mesh: dp: 64 (over z, x, core), tp: 4 (over y).
Axes of the slice: x: 4, y: 4, z: 8, core: 2. Of those that a mesh axis runs over, the one named last changes fastest.
Arguments:
- hidden: bfloat16 [2048, 4096], P('dp', 'tp'), may hold values from -6 to 6
- routes: int32 [2048, 8], P('dp'), may hold values from 0 to 63, all different within a row; in each aligned block of 32 rows (0 to 31, 32 to 63, ...) at most 8 rows name the same one
- routing_weights: float32 [2048, 8], P('dp'), may hold values from 0.05 to 1
- w_gate: bfloat16 [64, 4096, 1536], P('dp', None, 'tp'), may hold values from -0.09375 to 0.09375
- w_up: bfloat16 [64, 4096, 1536], P('dp', None, 'tp'), may hold values from -0.09375 to 0.09375
- w_down: bfloat16 [64, 1536, 4096], P('dp', 'tp'), may hold values from -0.15625 to 0.15625
- norm_gain: float32 [4096], replicated, may hold values from 0.1 to 1.9
- key_projection_weight: bfloat16 [4096, 512], P(None, 'tp'), may hold values from -0.09375 to 0.09375
- value_projection_weight: bfloat16 [4096, 512], P(None, 'tp'), may hold values from -0.09375 to 0.09375
- queries: bfloat16 [2048, 8192], P('dp', 'tp'), may hold values from -128 to 128
- cached_key_rows: bfloat16 [64, 128, 512], P('dp', None, 'tp'), may hold values from -4 to 4
- cached_value_rows: bfloat16 [64, 128, 512], P('dp', None, 'tp'), may hold values from -6 to 6
- lengths: int32 [64], P('dp'), may hold values from 16 to 128
- parents: int32 [64, 32], P('dp'), may hold values from -1 to 30, as said below
Outputs:
- layer_output: bfloat16 [2048, 4096], P('dp', 'tp')
- next_layer_keys: bfloat16 [2048, 512], P('dp', 'tp')
- next_layer_values: bfloat16 [2048, 512], P('dp', 'tp')
- attended: bfloat16 [2048, 8192], P('dp', 'tp')
Inputs may be any that keep to these rules, and one draw needn't show every extreme that they name: `routes`: each row names 8 different experts. In each aligned block of 32 rows (the rows of one device) no expert is named by more than 8 rows, a bound that some block reaches. `parents`: node 0 of each request is the root, with parent -1; every other node i has its parent among nodes max(0, i - 8) to i - 1.
All inputs are finite; a program needn't handle non-finite values.
Results may differ from a plain program's by a relative error of at most 0.013.
Values may be sent and summed in bfloat16 or wider, within the bound.
No kernel may reach another device: no remote copies, remote signals or barrier semaphores. Data moves between devices by JAX's collectives and lax.ppermute only.
A program may use at most 64 MiB of HBM per device.

v0:
```python
import math
import jax
import jax.numpy as jnp
from jax import lax
from jax.sharding import PartitionSpec as P

HEAD_SIZE = 128


def split_up(shard, dim, size):
    shape = shard.shape
    tiles = shard.reshape(*shape[:dim], size, shape[dim] // size, *shape[dim + 1 :])
    return jnp.moveaxis(tiles, dim, 0)


def sent_and_summed(shard, axis, dim):
    size = lax.axis_size(axis)
    tiles = lax.all_to_all(split_up(shard, dim, size), axis, 0, 0, tiled=True)
    return jnp.sum(tiles.astype(jnp.float32), axis=0)


def joined_along(tiles, dim):
    shape = list(tiles.shape[1:])
    shape[dim] *= tiles.shape[0]
    return jnp.moveaxis(tiles, 0, dim).reshape(shape)


def copy_for_each(shard, axis):
    copies = jnp.broadcast_to(shard, (lax.axis_size(axis), *shard.shape))
    return lax.all_to_all(copies, axis, split_axis=0, concat_axis=0, tiled=True)


def gathered_copies(shard, axis, dim):
    return joined_along(copy_for_each(shard, axis), dim)


def ancestry(parent_row):
    node_count = parent_row.shape[0]
    position = jnp.arange(node_count, dtype=jnp.int32)
    reached = (parent_row[:, None] == position[None, :]).astype(jnp.float32)
    reached = reached + jnp.eye(node_count, dtype=jnp.float32)
    for doubling in range((node_count - 1).bit_length()):
        reached = jnp.minimum(jnp.dot(reached, reached, preferred_element_type=jnp.float32), 1.0)
    return reached > 0.5


def quarter_to_whole(received):
    return lax.all_gather(received, "tp", axis=2, tiled=True)


def attend_local(
    queries, cached_key_rows, cached_value_rows, tree_key_rows, tree_value_rows, lengths, parents
):
    request_count = lengths.shape[0]
    node_count = parents.shape[1]
    slot_length = cached_key_rows.shape[1]
    kv_local = cached_key_rows.shape[2] // HEAD_SIZE
    query_group_count = queries.shape[1] // (kv_local * HEAD_SIZE)
    scaled = 1.0 / math.sqrt(HEAD_SIZE)
    tree_query_block = queries.reshape(
        request_count, node_count, kv_local, query_group_count, HEAD_SIZE
    )
    joined_key_block = cached_key_rows.reshape(request_count, slot_length, kv_local, HEAD_SIZE)
    joined_value_block = cached_value_rows.reshape(request_count, slot_length, kv_local, HEAD_SIZE)
    tree_key_block = tree_key_rows.reshape(request_count, node_count, kv_local, HEAD_SIZE)
    tree_value_block = tree_value_rows.reshape(request_count, node_count, kv_local, HEAD_SIZE)
    cache_scores = (
        jnp.einsum(
            "rnkgd,rpkd->rkgnp",
            tree_query_block,
            joined_key_block,
            preferred_element_type=jnp.float32,
        )
        * scaled
    )
    tree_scores = (
        jnp.einsum(
            "rnkgd,rmkd->rkgnm",
            tree_query_block,
            tree_key_block,
            preferred_element_type=jnp.float32,
        )
        * scaled
    )
    visible = jnp.arange(slot_length, dtype=jnp.int32)[None, :] < lengths[:, None]
    cache_scores = jnp.where(visible[:, None, None, None, :], cache_scores, -1e30)
    related = jax.vmap(ancestry)(parents)
    tree_scores = jnp.where(related[:, None, None], tree_scores, -1e30)
    highest = jnp.maximum(jnp.max(cache_scores, axis=-1), jnp.max(tree_scores, axis=-1))[..., None]
    cache_raised = jnp.exp(cache_scores - highest)
    tree_raised = jnp.exp(tree_scores - highest)
    denominator = jnp.sum(cache_raised, axis=-1, keepdims=True) + jnp.sum(
        tree_raised, axis=-1, keepdims=True
    )
    cache_weights = (cache_raised / denominator).astype(jnp.bfloat16)
    tree_weights = (tree_raised / denominator).astype(jnp.bfloat16)
    output = jnp.einsum(
        "rkgnp,rpkd->rnkgd", cache_weights, joined_value_block, preferred_element_type=jnp.float32
    )
    output = output + jnp.einsum(
        "rkgnm,rmkd->rnkgd", tree_weights, tree_value_block, preferred_element_type=jnp.float32
    )
    return output.reshape(request_count * node_count, -1).astype(jnp.bfloat16)


def on_device(
    hidden,
    routes,
    routing_weights,
    w_gate,
    w_up,
    w_down,
    norm_gain,
    key_projection_weight,
    value_projection_weight,
    queries,
    cached_key_rows,
    cached_value_rows,
    lengths,
    parents,
):
    token_count = hidden.shape[0]
    top_count = routes.shape[1]
    local_experts = w_gate.shape[0]
    expert_count = lax.axis_size("dp") * local_experts
    capacity = min(token_count, 2 * token_count * top_count // expert_count)
    column_count = hidden.shape[1]
    weights = routing_weights / jnp.sum(routing_weights, axis=1, keepdims=True)
    expert_ids = jnp.arange(expert_count, dtype=jnp.int32)
    chosen = routes[:, :, None] == expert_ids[None, None, :]
    member = jnp.any(chosen, axis=1)
    portion = jnp.sum(jnp.where(chosen, weights[:, :, None], 0.0), axis=1)
    earlier = jnp.tril(jnp.ones((token_count, token_count), jnp.bfloat16), -1)
    rank = jnp.dot(earlier, member.astype(jnp.bfloat16), preferred_element_type=jnp.float32)
    slots = jnp.arange(capacity, dtype=jnp.float32)
    placed = member.T[:, None, :] & (rank.T[:, None, :] == slots[None, :, None])
    placed = placed.reshape(expert_count * capacity, token_count)
    outgoing = jnp.dot(
        placed.astype(jnp.bfloat16), hidden, preferred_element_type=jnp.float32
    ).astype(jnp.bfloat16)
    outgoing = outgoing.reshape(expert_count, capacity, column_count)
    received = quarter_to_whole(
        lax.all_to_all(outgoing, "dp", split_axis=0, concat_axis=0, tiled=True)
    )
    slot_count = received.shape[1]
    grouped = received.reshape(-1, local_experts, slot_count, received.shape[2])
    gate_act = jnp.einsum("secd,edf->secf", grouped, w_gate, preferred_element_type=jnp.float32)
    upward = jnp.einsum("secd,edf->secf", grouped, w_up, preferred_element_type=jnp.float32)
    active = (jax.nn.silu(gate_act) * upward).astype(jnp.bfloat16)
    partial_value = jnp.einsum("secf,efd->secd", active, w_down, preferred_element_type=jnp.float32)
    partial_value = partial_value.reshape(received.shape[0], slot_count, partial_value.shape[3])
    summed = sent_and_summed(partial_value.astype(jnp.bfloat16), "tp", 2)
    back = lax.all_to_all(
        summed.astype(jnp.bfloat16), "dp", split_axis=0, concat_axis=0, tiled=True
    )
    flat_back = back.reshape(expert_count * capacity, back.shape[2])
    spread = jnp.broadcast_to(portion.T[:, None, :], (expert_count, capacity, token_count))
    spread = jnp.where(placed, spread.reshape(expert_count * capacity, token_count), 0.0)
    upper = spread.astype(jnp.bfloat16)
    lower = (spread - upper.astype(jnp.float32)).astype(jnp.bfloat16)
    both = jnp.concatenate([upper, lower], axis=1)
    mixed = lax.dot_general(
        both, flat_back, (((0,), (0,)), ((), ())), preferred_element_type=jnp.float32
    )
    expert_mix = mixed[:token_count] + mixed[token_count:]
    own_out = (hidden.astype(jnp.float32) + expert_mix).astype(jnp.bfloat16)
    full_out = gathered_copies(own_out, "tp", 1)
    widened = full_out.astype(jnp.float32)
    scaling = lax.rsqrt(jnp.mean(widened * widened, axis=1, keepdims=True) + 1e-06)
    normed = (widened * scaling * norm_gain).astype(jnp.bfloat16)
    tree_key_rows = jnp.dot(
        normed, key_projection_weight, preferred_element_type=jnp.float32
    ).astype(jnp.bfloat16)
    tree_value_rows = jnp.dot(
        normed, value_projection_weight, preferred_element_type=jnp.float32
    ).astype(jnp.bfloat16)
    attended = attend_local(
        queries,
        cached_key_rows,
        cached_value_rows,
        tree_key_rows,
        tree_value_rows,
        lengths,
        parents,
    )
    return (own_out, tree_key_rows, tree_value_rows, attended)


def solution(mesh):
    return jax.shard_map(
        on_device,
        mesh=mesh,
        in_specs=(
            P("dp", "tp"),
            P("dp", None),
            P("dp", None),
            P("dp", None, "tp"),
            P("dp", None, "tp"),
            P("dp", "tp", None),
            P(),
            P(None, "tp"),
            P(None, "tp"),
            P("dp", "tp"),
            P("dp", None, "tp"),
            P("dp", None, "tp"),
            P("dp"),
            P("dp", None),
        ),
        out_specs=(P("dp", "tp"), P("dp", "tp"), P("dp", "tp"), P("dp", "tp")),
        check_vma=False,
    )
```

profile of v0, /device:TPU:2, one launch (start us, length us, event | category | flops | bytes accessed | tf_op | source)
XLA Modules:
  0.0 239.4 jit_solution(4586139410621288270)
XLA Ops:
  7.2 0.0 copy-start
  7.2 0.0 all-gather.2.cloned.1.call-start
  7.2 0.9 copy.67
  8.2 0.7 reduce_sum.57
  8.9 0.7 broadcast_divide_fusion
  9.5 0.1 copy.72
  9.6 0.1 fusion.45
  9.8 0.1 select_reduce_fusion
  9.9 0.1 copy.73
  10.0 0.1 copy.74
  10.1 0.2 fusion.55
  10.3 0.1 copy.70
  10.5 0.1 copy.68
  10.6 0.1 copy.71
  10.7 0.1 eq.96
  10.9 1.3 fusion.5
  12.2 40.7 %all_to_all.20 = bf16[64,8,1024]{2,1,0:T(8,128)(2,1)} all-to-all(bf16[64,8,1024]{2,1,0:T(8,128)(2,1)S(1)} %fusion.5), channel_id=1, replica_groups=mesh['dp'=64,'tp'=4] {'dp'}, dimensions={0} | all-to-all | bytes 2097152 | tf_op jit(solution)/shard_map/all_to_all | solution.py:143
  52.9 0.0 all-gather.2.cloned.1.call-update
  52.9 47.6 %all-gather.2.cloned.1.call-done = bf16[64,8,4096]{2,1,0:T(8,128)(2,1)} async-done(((bf16[64,8,1024]{2,1,0:T(8,128)(2,1)}), bf16[64,8,4096]{2,1,0:T(8,128)(2,1)}) %all-gather.2.cloned.1.call-update) | async-done | bytes 4194320 | tf_op jit(solution)/shard_map/all_gather | solution.py:48
  100.5 6.4 %fusion.6 = f32[64,1,8,384]{3,2,0,1:T(8,128)} fusion(bf16[64,8,4096]{2,1,0:T(8,128)(2,1)} %all-gather.2.cloned.1.call-done, bf16[1,4096,384]{2,1,0:T(8,128)(2,1)} %param.17), kind=kOutput, calls=%fused_computation.9 | convolution fusion | flops 1610612736 | bytes 8126464 | tf_op jit(solution)/shard_map/secd,edf->secf/dot_general | solution.py:147
  107.0 9.7 %convolution_convert_fusion = bf16[64,8,4096]{2,1,0:T(8,128)(2,1)} fusion(bf16[1,384,4096]{2,1,0:T(8,128)(2,1)S(1)} %copy-done, bf16[64,8,4096]{2,1,0:T(8,128)(2,1)} %all-gather.2.cloned.1.call-done, bf16[1,4096,384]{2,1,0:T(8,128)(2,1)} %param.18, f32[64,1,8,384]{3,2,0,1:T(8,128)} %fusion.6), kind=kOutput, calls=%fused_computation | convolution fusion | flops 3224502272 | bytes 15466496 | tf_op jit(solution)/shard_map/secf,efd->secd/dot_general | solution.py:150
  116.7 2.6 %copy.101 = bf16[64,8,4,1024]{3,1,0,2:T(8,128)(2,1)S(1)} copy(bf16[64,8,4,1024]{3,1,2,0:T(8,128)(2,1)} %bitcast.160) | data formatting | bytes 8388608 | tf_op jit(solution)/shard_map/convert_element_type | solution.py:152
  119.3 52.5 %all_to_all.21 = bf16[4,64,8,1024]{3,2,1,0:T(8,128)(2,1)} all-to-all(bf16[4,64,8,1024]{3,2,1,0:T(8,128)(2,1)S(1)} %bitcast.157), channel_id=1, replica_groups=mesh['dp'=64,'tp'=4] {'tp'}, dimensions={0} | all-to-all | bytes 8388608 | tf_op jit(solution)/shard_map/all_to_all | solution.py:18
  171.8 4.4 %reduce_sum.59 = bf16[64,8,1024]{2,1,0:T(8,128)(2,1)} reduce(bf16[4,64,8,1024]{3,2,1,0:T(8,128)(2,1)} %all_to_all.21, bf16[]{:T(256)} %constant.15.clone.1), dimensions={0}, to_apply=%region_3.4 | reduce | flops 1572864 | bytes 5242882 | tf_op jit(solution)/shard_map/reduce_sum | solution.py:19
  176.2 10.8 %all-to-all-start.2 = ((bf16[64,8,1024]{2,1,0:T(8,128)(2,1)}), bf16[64,8,1024]{2,1,0:T(8,128)(2,1)}, u32[]{:S(2)}, u32[]{:S(2)}) async-start(bf16[64,8,1024]{2,1,0:T(8,128)(2,1)} %reduce_sum.59), calls=%async_computation.2 | async-start | bytes 2097152 | tf_op jit(solution)/shard_map/all_to_all | solution.py:153
  187.1 0.1 fusion.53
  187.2 0.1 convolution_minimum_fusion.4
  187.3 0.2 convolution_minimum_fusion.2
  187.5 0.2 fusion.28
  187.8 0.7 copy.78
  189.1 0.5 iota_compare_fusion.2
  189.7 26.1 %all-to-all-done.2 = bf16[64,8,1024]{2,1,0:T(8,128)(2,1)} async-done(((bf16[64,8,1024]{2,1,0:T(8,128)(2,1)}), bf16[64,8,1024]{2,1,0:T(8,128)(2,1)}, u32[]{:S(2)}, u32[]{:S(2)}) %all-to-all-start.2) | async-done | bytes 1048608 | tf_op jit(solution)/shard_map/all_to_all | solution.py:153
  215.8 1.6 fusion.29
  217.4 0.0 copy-start.5
  217.4 0.7 broadcast_in_dim.81
  218.1 3.4 %all-to-all-start.3 = ((bf16[4,32,1024]{2,1,0:T(8,128)(2,1)}), bf16[4,32,1024]{2,1,0:T(8,128)(2,1)S(1)}, u32[]{:S(2)}, u32[]{:S(2)}) async-start(bf16[4,32,1024]{2,1,0:T(8,128)(2,1)} %broadcast_in_dim.81), calls=%async_computation.3 | async-start | bytes 524288 | tf_op jit(solution)/shard_map/all_to_all | solution.py:30
  221.5 2.4 %fusion.71 = (f32[16,32]{1,0:T(8,128)}, f32[1,1,16,32,128]{4,3,2,1,0:T(8,128)}) fusion(bf16[1,128,128]{2,1,0:T(8,128)(2,1)} %param.24, pred[128]{0:T(512)(128)(4,1)} %iota_compare_fusion.2, bf16[32,2048]{1,0:T(8,128)(2,1)} %param.23), kind=kOutput, calls=%fused_computation.96 | convolution fusion | flops 16973312 | bytes 428160 | tf_op jit(solution)/shard_map/rnkgd,rpkd->rkgnp/dot_general | solution.py:68
  223.9 4.2 %all-to-all-done.3 = bf16[4,32,1024]{2,1,0:T(8,128)(2,1)S(1)} async-done(((bf16[4,32,1024]{2,1,0:T(8,128)(2,1)}), bf16[4,32,1024]{2,1,0:T(8,128)(2,1)S(1)}, u32[]{:S(2)}, u32[]{:S(2)}) %all-to-all-start.3) | async-done | bytes 262176 | tf_op jit(solution)/shard_map/all_to_all | solution.py:30
  228.3 0.2 fusion.33
  228.5 1.7 convolution_convert_fusion.3
  230.2 0.3 fusion.72
  230.5 0.1 fusion.36
  230.6 0.3 fusion.35
  230.9 0.3 convolution_convert_fusion.2
  231.3 0.3 convolution_bitcast_fusion
  231.6 0.3 fusion.27
  231.8 0.1 copy.81
  231.9 0.7 copy.102
  (37 shorter events, 0.3 us)
Async XLA Ops:
  7.2 99.8 %copy-start = (bf16[1,384,4096]{2,1,0:T(8,128)(2,1)S(1)}, bf16[1,384,4096]{2,1,0:T(8,128)(2,1)}, u32[]{:S(2)}) copy-start(bf16[1,384,4096]{2,1,0:T(8,128)(2,1)} %param.19) | copy-start | bytes 9437188
  7.2 93.3 %all-gather.2.cloned.1.call-start = ((), (), s32[]{:S(2)}) async-start(), calls=%async_computation.4 | async-start | bytes 5242880 | tf_op jit(solution)/shard_map/all_gather | solution.py:48
  171.8 15.3 %copy-start.11 = (s32[1,32]{1,0:T(1,128)S(1)}, s32[1,32]{1,0:T(1,128)}, u32[]{:S(2)}) copy-start(s32[1,32]{1,0:T(1,128)} %param.27) | copy-start | bytes 388
  176.2 41.1 %copy-start.4 = (bf16[32,1024]{1,0:T(8,128)(2,1)S(1)}, bf16[32,1024]{1,0:T(8,128)(2,1)}, u32[]{:S(2)}) copy-start(bf16[32,1024]{1,0:T(8,128)(2,1)} %param.14) | copy-start | bytes 196612
  176.2 39.6 %all-to-all-start.2 = ((bf16[64,8,1024]{2,1,0:T(8,128)(2,1)}), bf16[64,8,1024]{2,1,0:T(8,128)(2,1)}, u32[]{:S(2)}, u32[]{:S(2)}) async-start(bf16[64,8,1024]{2,1,0:T(8,128)(2,1)} %reduce_sum.59), calls=%async_computation.2 | async-start | bytes 2097152 | tf_op jit(solution)/shard_map/all_to_all | solution.py:153
  187.0 41.4 %copy-start.6 = (f32[4096]{0:T(1024)S(1)}, f32[4096]{0:T(1024)}, u32[]{:S(2)}) copy-start(f32[4096]{0:T(1024)} %param.20) | copy-start | bytes 49156
  215.8 14.4 %copy-start.3 = (bf16[32,2048]{1,0:T(8,128)(2,1)S(1)}, bf16[32,2048]{1,0:T(8,128)(2,1)}, u32[]{:S(2)}) copy-start(bf16[32,2048]{1,0:T(8,128)(2,1)} %param.23) | copy-start | bytes 393220
  217.4 0.7 copy-start.5
  218.1 10.1 %all-to-all-start.3 = ((bf16[4,32,1024]{2,1,0:T(8,128)(2,1)}), bf16[4,32,1024]{2,1,0:T(8,128)(2,1)S(1)}, u32[]{:S(2)}, u32[]{:S(2)}) async-start(bf16[4,32,1024]{2,1,0:T(8,128)(2,1)} %broadcast_in_dim.81), calls=%async_computation.3 | async-start | bytes 524288 | tf_op jit(solution)/shard_map/all_to_all | solution.py:30
  228.2 2.0 copy-start.9
  228.2 2.4 copy-start.8
  228.2 2.5 %copy-start.2 = (f32[1,1,16,32,128]{4,3,2,1,0:T(8,128)S(1)}, f32[1,1,16,32,128]{4,3,2,1,0:T(8,128)}, u32[]{:S(2)}) copy-start(f32[1,1,16,32,128]{4,3,2,1,0:T(8,128)} %get-tuple-element.7) | copy-start | bytes 786436
  228.2 2.7 %copy-start.1 = (bf16[4096,128]{1,0:T(8,128)(2,1)S(1)}, bf16[4096,128]{1,0:T(8,128)(2,1)}, u32[]{:S(2)}) copy-start(bf16[4096,128]{1,0:T(8,128)(2,1)} %param.22) | copy-start | bytes 3145732
  228.2 3.1 %copy-start.12 = (bf16[1,128,128]{2,1,0:T(8,128)(2,1)S(1)}, bf16[1,128,128]{2,1,0:T(8,128)(2,1)}, u32[]{:S(2)}) copy-start(bf16[1,128,128]{2,1,0:T(8,128)(2,1)} %param.25) | copy-start | bytes 98308
  230.2 2.4 %copy-start.7 = (bf16[32,128]{1,0:T(8,128)(2,1)}, bf16[32,128]{1,0:T(8,128)(2,1)S(1)}, u32[]{:S(2)}) copy-start(bf16[32,128]{1,0:T(8,128)(2,1)S(1)} %convolution_convert_fusion.3) | copy-start | bytes 24580
  231.2 1.4 copy-start.10
Sparse Core Ops, SparseCore 0:
  53.0 47.4 all-gather.1
where the time goes:
time: 240 us; the launch traced here: 239 us
  blocking collectives  93.2 us (39%)
  waiting for transfers between devices  77.9 us (32%)
  matrix products  25.2 us (10%)
  between operations  15 us (6%)
  starting transfers between devices  14.3 us (6%)
  other arithmetic  7.3 us (3%)
  local copies, waits for them, and re-layouts  6.57 us (3%)
    all_to_all x1, blocking collectives, sent_and_summed(): tiles = lax.all_to_all(split_up(shard, dim, size), axis, 0, 0, tiled=True)  52.5 us
    all_gather x1, waiting for transfers between devices, quarter_to_whole(): return lax.all_gather(received, 'tp', axis=2, tiled=True)  47.6 us
    all_to_all x1, blocking collectives, on_device(): lax.all_to_all(outgoing, 'dp', split_axis=0, concat_axis=0, tiled=True)  40.7 us
    all_to_all x1, waiting for transfers between devices, on_device(): lax.all_to_all(summed.astype(jnp.bfloat16), 'dp', split_axis=0, concat_ax...  26.1 us
    all_to_all x1, starting transfers between devices, on_device(): lax.all_to_all(summed.astype(jnp.bfloat16), 'dp', split_axis=0, concat_ax...  10.8 us
    dot_general x1, matrix products, on_device(): jnp.einsum('secf,efd->secd', active, w_down, preferred_element_type=jnp.f...  9.74 us
    dot_general x1, matrix products, on_device(): jnp.einsum('secd,edf->secf', grouped, w_gate, preferred_element_type=jnp....  6.43 us
  transfers between devices with their start and end apart: 3, of which 3 were waited for; matrix products, arithmetic and copies ran while one was open for 2% of the time, Pallas kernels for 0%

commit v1 on v0

--- a/solution.py
+++ b/solution.py
@@ -3,6 +3,7 @@
 import jax.numpy as jnp
 from jax import lax
 from jax.sharding import PartitionSpec as P
+from jax.lax import all_to_all, axis_size
 
 HEAD_SIZE = 128
 
@@ -45,7 +46,15 @@
 
 
 def quarter_to_whole(received):
-    return lax.all_gather(received, "tp", axis=2, tiled=True)
+
+    def post_circles(mesh_dim, own_rows):
+        cores_n = axis_size(mesh_dim)
+        row_list = [cores_n if w == 2 else 1 for w in range(own_rows.ndim)]
+        a_now = jnp.tile(own_rows, row_list)
+        local_now = all_to_all(a_now, mesh_dim, split_axis=2, concat_axis=2, tiled=True)
+        return local_now
+
+    return post_circles("tp", received)
 
 
 def attend_local(

time: 240 us -> 271 us (1.13)
  blocking collectives: 93.2 us -> 145 us
  waiting for transfers between devices: 77.9 us -> 32 us
  local copies, waits for them, and re-layouts: 6.57 us -> 46.8 us
  between operations: 15 us -> 1.59 us
    all_to_all x0 -> x1, blocking collectives: none -> 53.9 us  [post_circles(): all_to_all(a_now, mesh_dim, split_axis=2, concat_axis=2, tiled=True)]
    all_gather x1 -> x0, waiting for transfers between devices: 47.6 us -> none  [quarter_to_whole(): return lax.all_gather(received, 'tp', axis=2, tiled=True)]
    unnamed x28 -> x26, local copies, waits for them, and re-layouts: 1.67 us -> 20.4 us
    all_to_all x0 -> x2, local copies, waits for them, and re-layouts: none -> 16.2 us  [the longest x1 12 us: post_circles(): all_to_all(a_now, mesh_dim, split_axis=2, concat_axis=2, tiled=True)]
    another operation x0 -> x1, local copies, waits for them, and re-layouts: none -> 5.89 us  [post_circles(): a_now = jnp.tile(own_rows, row_list)]
  transfers between devices with their start and end apart: 3 -> 2, of which waited for: 3 -> 2; matrix products, arithmetic and copies ran while one was open for 2% -> 1% of each run, Pallas kernels for 0% -> 0%
where the time goes in v1:
time: 271 us; the launch traced here: 270 us
  blocking collectives  145 us (54%)
  local copies, waits for them, and re-layouts  46.8 us (17%)
  waiting for transfers between devices  32 us (12%)
  matrix products  25.4 us (9%)
  starting transfers between devices  11.6 us (4%)
  other arithmetic  6.83 us (3%)
    all_to_all x1, blocking collectives, post_circles(): all_to_all(a_now, mesh_dim, split_axis=2, concat_axis=2, tiled=True)  53.9 us
    all_to_all x1, blocking collectives, sent_and_summed(): tiles = lax.all_to_all(split_up(shard, dim, size), axis, 0, 0, tiled=True)  50.7 us
    all_to_all x1, blocking collectives, on_device(): lax.all_to_all(outgoing, 'dp', split_axis=0, concat_axis=0, tiled=True)  40.7 us
    all_to_all x1, waiting for transfers between devices, on_device(): lax.all_to_all(summed.astype(jnp.bfloat16), 'dp', split_axis=0, concat_ax...  27.2 us
    unnamed x26, local copies, waits for them, and re-layouts  20.4 us
    all_to_all x1, local copies, waits for them, and re-layouts, post_circles(): all_to_all(a_now, mesh_dim, split_axis=2, concat_axis=2, tiled=True)  12 us
    dot_general x1, matrix products, on_device(): jnp.einsum('secf,efd->secd', active, w_down, preferred_element_type=jnp.f...  9.73 us
    all_to_all x1, starting transfers between devices, on_device(): lax.all_to_all(summed.astype(jnp.bfloat16), 'dp', split_axis=0, concat_ax...  8.2 us
  transfers between devices with their start and end apart: 2, of which 2 were waited for; matrix products, arithmetic and copies ran while one was open for 1% of the time, Pallas kernels for 0%

profile of v1, /device:TPU:2, one launch (start us, length us, event | category | flops | bytes accessed | tf_op | source)
XLA Modules:
  0.0 269.6 jit_solution(13264621185390337528)
XLA Ops:
  0.7 0.9 copy.90
  1.6 0.7 reduce_sum.57
  2.3 0.7 broadcast_divide_fusion
  3.0 0.1 copy.95
  3.1 0.1 fusion.45
  3.2 0.1 select_reduce_fusion
  3.4 0.1 copy.96
  3.5 0.1 copy.97
  3.6 0.2 fusion.55
  3.8 0.1 copy.93
  3.9 0.1 copy.91
  4.0 0.1 copy.94
  4.2 0.1 eq.96
  4.3 1.3 fusion.5
  5.6 40.7 %all_to_all.25 = bf16[64,8,1024]{2,1,0:T(8,128)(2,1)} all-to-all(bf16[64,8,1024]{2,1,0:T(8,128)(2,1)S(1)} %fusion.5), channel_id=1, replica_groups=mesh['dp'=64,'tp'=4] {'dp'}, dimensions={0} | all-to-all | bytes 2097152 | tf_op jit(solution)/shard_map/all_to_all | solution.py:152
  46.3 4.2 %copy.98 = bf16[64,8,1024]{0,1,2:T(8,128)(2,1)} copy(bf16[64,8,1024]{2,1,0:T(8,128)(2,1)} %all_to_all.25) | data formatting | bytes 2097152 | tf_op jit(solution)/shard_map/all_to_all | solution.py:152
  50.5 5.9 %tile.4 = bf16[64,8,4,1024]{0,1,3,2:T(8,128)(2,1)} broadcast(bf16[64,8,1024]{0,1,2:T(8,128)(2,1)} %copy.98), dimensions={0,1,3} | broadcast | bytes 5242880 | tf_op jit(solution)/shard_map/tile | solution.py:53
  56.4 9.5 %reshape.325 = bf16[4,2,262144]{2,1,0:T(2,128)(2,1)} reshape(bf16[4096,8,64]{2,1,0:T(8,128)(2,1)} %bitcast.160) | data formatting | bytes 8388608
  65.9 53.9 %all_to_all.26 = bf16[4,2,262144]{2,1,0:T(2,128)(2,1)} all-to-all(bf16[4,2,262144]{2,1,0:T(2,128)(2,1)} %reshape.325), channel_id=1, replica_groups=mesh['dp'=64,'tp'=4] {'tp'}, dimensions={0} | all-to-all | bytes 8388608 | tf_op jit(solution)/shard_map/all_to_all | solution.py:54
  119.8 9.2 %reshape.326 = bf16[4096,8,64]{2,1,0:T(8,128)(2,1)} reshape(bf16[4,2,262144]{2,1,0:T(2,128)(2,1)} %all_to_all.26) | data formatting | bytes 8388608
  129.1 12.0 %copy.99 = bf16[64,8,4096]{2,1,0:T(8,128)(2,1)} copy(bf16[64,8,4096]{0,1,2:T(8,128)(2,1)} %bitcast.161) | data formatting | bytes 8388608 | tf_op jit(solution)/shard_map/all_to_all | solution.py:54
  141.1 6.4 %fusion.6 = f32[64,1,8,384]{3,2,0,1:T(8,128)} fusion(bf16[64,8,4096]{2,1,0:T(8,128)(2,1)} %copy.99, bf16[1,4096,384]{2,1,0:T(8,128)(2,1)} %param.17), kind=kOutput, calls=%fused_computation.9 | convolution fusion | flops 1610612736 | bytes 8126464 | tf_op jit(solution)/shard_map/secd,edf->secf/dot_general | solution.py:156
  147.5 9.7 %convolution_convert_fusion = bf16[64,8,4096]{2,1,0:T(8,128)(2,1)} fusion(bf16[1,384,4096]{2,1,0:T(8,128)(2,1)S(1)} %copy-done, bf16[64,8,4096]{2,1,0:T(8,128)(2,1)} %copy.99, bf16[1,4096,384]{2,1,0:T(8,128)(2,1)} %param.18, f32[64,1,8,384]{3,2,0,1:T(8,128)} %fusion.6), kind=kOutput, calls=%fused_computation | convolution fusion | flops 3224502272 | bytes 15466496 | tf_op jit(solution)/shard_map/secf,efd->secd/dot_general | solution.py:159
  157.2 2.6 copy.127
  159.9 50.7 %all_to_all.27 = bf16[4,64,8,1024]{3,2,1,0:T(8,128)(2,1)} all-to-all(bf16[4,64,8,1024]{3,2,1,0:T(8,128)(2,1)S(1)} %bitcast.162), channel_id=1, replica_groups=mesh['dp'=64,'tp'=4] {'tp'}, dimensions={0} | all-to-all | bytes 8388608 | tf_op jit(solution)/shard_map/all_to_all | solution.py:19
  210.6 4.4 %reduce_sum.59 = bf16[64,8,1024]{2,1,0:T(8,128)(2,1)} reduce(bf16[4,64,8,1024]{3,2,1,0:T(8,128)(2,1)} %all_to_all.27, bf16[]{:T(256)} %constant.15.clone.1), dimensions={0}, to_apply=%region_3.4 | reduce | flops 1572864 | bytes 5242882 | tf_op jit(solution)/shard_map/reduce_sum | solution.py:20
  215.0 8.2 %all-to-all-start.3 = ((bf16[64,8,1024]{2,1,0:T(8,128)(2,1)}), bf16[64,8,1024]{2,1,0:T(8,128)(2,1)}, u32[]{:S(2)}, u32[]{:S(2)}) async-start(bf16[64,8,1024]{2,1,0:T(8,128)(2,1)} %reduce_sum.59), calls=%async_computation.3 | async-start | bytes 2097152 | tf_op jit(solution)/shard_map/all_to_all | solution.py:162
  223.2 0.1 fusion.53
  223.3 0.1 convolution_minimum_fusion.4
  223.4 0.2 convolution_minimum_fusion.2
  223.7 0.2 fusion.28
  223.9 0.1 copy.104
  224.7 27.2 %all-to-all-done.3 = bf16[64,8,1024]{2,1,0:T(8,128)(2,1)} async-done(((bf16[64,8,1024]{2,1,0:T(8,128)(2,1)}), bf16[64,8,1024]{2,1,0:T(8,128)(2,1)}, u32[]{:S(2)}, u32[]{:S(2)}) %all-to-all-start.3) | async-done | bytes 1048608 | tf_op jit(solution)/shard_map/all_to_all | solution.py:162
  251.9 1.5 fusion.29
  253.5 0.7 broadcast_in_dim.81
  254.2 3.4 %all-to-all-start.4 = ((bf16[4,32,1024]{2,1,0:T(8,128)(2,1)}), bf16[4,32,1024]{2,1,0:T(8,128)(2,1)S(1)}, u32[]{:S(2)}, u32[]{:S(2)}) async-start(bf16[4,32,1024]{2,1,0:T(8,128)(2,1)} %broadcast_in_dim.81), calls=%async_computation.4 | async-start | bytes 524288 | tf_op jit(solution)/shard_map/all_to_all | solution.py:31
  257.6 1.8 fusion.71
  259.4 4.8 %all-to-all-done.4 = bf16[4,32,1024]{2,1,0:T(8,128)(2,1)S(1)} async-done(((bf16[4,32,1024]{2,1,0:T(8,128)(2,1)}), bf16[4,32,1024]{2,1,0:T(8,128)(2,1)S(1)}, u32[]{:S(2)}, u32[]{:S(2)}) %all-to-all-start.4) | async-done | bytes 262176 | tf_op jit(solution)/shard_map/all_to_all | solution.py:31
  264.4 0.2 fusion.33
  264.5 1.7 convolution_convert_fusion.3
  266.2 1.2 fusion.72
  267.5 0.1 fusion.36
  267.6 0.3 fusion.35
  267.9 0.3 convolution_convert_fusion.2
  268.2 0.3 convolution_bitcast_fusion
  268.5 0.3 fusion.27
  268.8 0.1 copy.107
  268.9 0.7 copy.128
  (36 shorter events, 0.3 us)
Async XLA Ops:
  0.6 146.9 %copy-start = (bf16[1,384,4096]{2,1,0:T(8,128)(2,1)S(1)}, bf16[1,384,4096]{2,1,0:T(8,128)(2,1)}, u32[]{:S(2)}) copy-start(bf16[1,384,4096]{2,1,0:T(8,128)(2,1)} %param.19) | copy-start | bytes 9437188
  210.6 12.6 %copy-start.9 = (s32[1,32]{1,0:T(1,128)S(1)}, s32[1,32]{1,0:T(1,128)}, u32[]{:S(2)}) copy-start(s32[1,32]{1,0:T(1,128)} %param.27) | copy-start | bytes 388
  210.6 42.9 %copy-start.3 = (bf16[32,1024]{1,0:T(8,128)(2,1)S(1)}, bf16[32,1024]{1,0:T(8,128)(2,1)}, u32[]{:S(2)}) copy-start(bf16[32,1024]{1,0:T(8,128)(2,1)} %param.14) | copy-start | bytes 196612
  210.6 47.0 %copy-start.7 = (bf16[1,128,128]{2,1,0:T(8,128)(2,1)S(1)}, bf16[1,128,128]{2,1,0:T(8,128)(2,1)}, u32[]{:S(2)}) copy-start(bf16[1,128,128]{2,1,0:T(8,128)(2,1)} %param.24) | copy-start | bytes 98308
  215.0 49.6 %copy-start.5 = (f32[4096]{0:T(1024)S(1)}, f32[4096]{0:T(1024)}, u32[]{:S(2)}) copy-start(f32[4096]{0:T(1024)} %param.20) | copy-start | bytes 49156
  215.0 36.9 %all-to-all-start.3 = ((bf16[64,8,1024]{2,1,0:T(8,128)(2,1)}), bf16[64,8,1024]{2,1,0:T(8,128)(2,1)}, u32[]{:S(2)}, u32[]{:S(2)}) async-start(bf16[64,8,1024]{2,1,0:T(8,128)(2,1)} %reduce_sum.59), calls=%async_computation.3 | async-start | bytes 2097152 | tf_op jit(solution)/shard_map/all_to_all | solution.py:162
  253.5 15.1 %copy-start.4 = (bf16[32,1024]{1,0:T(8,128)(2,1)}, bf16[32,1024]{1,0:T(8,128)(2,1)S(1)}, u32[]{:S(2)}) copy-start(bf16[32,1024]{1,0:T(8,128)(2,1)S(1)} %fusion.40) | copy-start | bytes 196612
  254.2 10.1 %all-to-all-start.4 = ((bf16[4,32,1024]{2,1,0:T(8,128)(2,1)}), bf16[4,32,1024]{2,1,0:T(8,128)(2,1)S(1)}, u32[]{:S(2)}, u32[]{:S(2)}) async-start(bf16[4,32,1024]{2,1,0:T(8,128)(2,1)} %broadcast_in_dim.81), calls=%async_computation.4 | async-start | bytes 524288 | tf_op jit(solution)/shard_map/all_to_all | solution.py:31
  264.3 3.3 %copy-start.2 = (f32[1,1,16,32,128]{4,3,2,1,0:T(8,128)S(1)}, f32[1,1,16,32,128]{4,3,2,1,0:T(8,128)}, u32[]{:S(2)}) copy-start(f32[1,1,16,32,128]{4,3,2,1,0:T(8,128)} %get-tuple-element.7) | copy-start | bytes 786436
  264.3 3.6 %copy-start.1 = (bf16[4096,128]{1,0:T(8,128)(2,1)S(1)}, bf16[4096,128]{1,0:T(8,128)(2,1)}, u32[]{:S(2)}) copy-start(bf16[4096,128]{1,0:T(8,128)(2,1)} %param.22) | copy-start | bytes 3145732
  264.3 3.9 %copy-start.10 = (bf16[1,128,128]{2,1,0:T(8,128)(2,1)S(1)}, bf16[1,128,128]{2,1,0:T(8,128)(2,1)}, u32[]{:S(2)}) copy-start(bf16[1,128,128]{2,1,0:T(8,128)(2,1)} %param.25) | copy-start | bytes 98308
  266.2 3.3 %copy-start.6 = (bf16[32,128]{1,0:T(8,128)(2,1)}, bf16[32,128]{1,0:T(8,128)(2,1)S(1)}, u32[]{:S(2)}) copy-start(bf16[32,128]{1,0:T(8,128)(2,1)S(1)} %convolution_convert_fusion.3) | copy-start | bytes 24580
  268.2 1.4 copy-start.8
